TPU v7x, 256 devices: a whole 4x4x8 slice. The times are simulated.
256 devices in a mesh: rel: 16 (over x, y), node: 16 (over z, core).
Axes of the slice: x: 4, y: 4, z: 8, core: 2. Of those that a mesh axis runs over, the one named last changes fastest.
Arguments:
- out_adjoint: bfloat16 [16, 1024, 512], P('node', 'rel'), may hold values from -6 to 6
- layer_input: bfloat16 [16, 1024, 512], P('node'), may hold values from -0.15625 to 0.15625
- rel_weights: bfloat16 [32, 512, 512], P('rel'), may hold values from -0.25 to 0.25
- self_weight: bfloat16 [512, 512], replicated, may hold values from -0.25 to 0.25
- tile_values: bfloat16 [16, 1024, 128, 128], P('rel', 'node'), may hold values from 0 to 0.039794922
- tile_rel: int32 [16, 1024], P('rel', 'node'), may hold values from 0 to 1
- tile_target: int32 [16, 1024], P('rel', 'node'), may hold values from 0 to 7
- tile_src: int32 [16, 1024], P('rel', 'node'), may hold values from 0 to 7
- tile_dest: int32 [16, 1024, 1], P('rel', 'node'), may hold values from 0 to 15; in each aligned block of 64 rows (0 to 63, 64 to 127, ..., all dimensions but the last counted through in order) at most 8 rows name the same one
Outputs:
- rel_weight_grad: float32 [32, 512, 512], P('rel', 'node')
- d_source: bfloat16 [16, 1024, 512], P('node', 'rel')
Inputs may be any that keep to these rules, and one draw needn't show every extreme that they name: `tile_dest`: among the 64 tiles of one device, at most 8 name the same node shard, and some node shard is named by exactly 8 of them.
All inputs are finite; a program needn't handle non-finite values.
Results may differ from a plain program's by a relative error of at most 0.0056.
Values may be sent and summed in bfloat16 or wider, within the bound.
A program may use at most 128 MiB of HBM per device.

v0:
```python
import jax
import jax.numpy as jnp
from jax import lax
from jax.sharding import PartitionSpec as P


def on_device(
    out_adjoint,
    layer_input,
    rel_weights,
    self_weight,
    tile_values,
    tile_rel,
    tile_target,
    tile_src,
    tile_dest,
):
    shard_count = lax.axis_size("node")
    tile_edge = tile_values.shape[-1]
    row_count = layer_input.shape[1]
    feature = layer_input.shape[2]
    blocks = row_count // tile_edge
    relations = rel_weights.shape[0]
    tile_count = tile_values.shape[1]
    capacity = 2 * tile_count // shard_count
    slot_count = shard_count * capacity
    adjoint = lax.all_gather(out_adjoint, "rel", axis=1, tiled=True)[0]
    owners = tile_dest[0, :, 0]
    relation = tile_rel[0]
    target = tile_target[0]
    source = tile_src[0]
    shared = owners[:, None] == owners[None, :]
    indices = jnp.arange(tile_count)
    earlier = indices[None, :] < indices[:, None]
    position = jnp.sum(jnp.logical_and(shared, earlier).astype(jnp.int32), axis=1)
    slot_of = owners * capacity + position
    placed = jnp.arange(slot_count)[:, None] == slot_of[None, :]
    placing = placed.astype(jnp.bfloat16)
    group_rows = lax.all_gather(adjoint[None], "node", axis=0, tiled=True)
    packed = relation * (blocks * blocks) + target * blocks + source
    outgoing = jnp.dot(
        placing,
        tile_values[0].reshape(tile_count, tile_edge * tile_edge),
        preferred_element_type=jnp.float32,
    )
    outgoing = outgoing.astype(jnp.bfloat16).reshape(shard_count, capacity, tile_edge, tile_edge)
    packed_slots = jnp.sum(jnp.where(placed, packed[None, :], 0), axis=1).reshape(
        shard_count, capacity
    )
    got_tiles, got_packed = (
        lax.all_to_all(outgoing, "node", split_axis=0, concat_axis=0, tiled=True),
        lax.all_to_all(packed_slots, "node", split_axis=0, concat_axis=0, tiled=True),
    )
    got_packed = got_packed.reshape(slot_count)
    got_target = got_packed // blocks % blocks
    bucket = got_packed // (blocks * blocks) * blocks + got_packed % blocks
    sender = jnp.arange(slot_count) // capacity
    chosen = jnp.take(
        group_rows.reshape(shard_count * blocks, tile_edge, feature),
        sender * blocks + got_target,
        axis=0,
    )
    partial_value = jnp.einsum(
        "sij,sid->sjd",
        got_tiles.reshape(slot_count, tile_edge, tile_edge),
        chosen,
        preferred_element_type=jnp.float32,
    )
    partial_value = partial_value.astype(jnp.bfloat16)
    onehot = (bucket[:, None] == jnp.arange(relations * blocks)[None, :]).astype(jnp.bfloat16)
    summed = jnp.einsum(
        "sk,sx->kx",
        onehot,
        partial_value.reshape(slot_count, tile_edge * feature),
        preferred_element_type=jnp.float32,
    )
    aggregated = summed.reshape(relations, row_count, feature).astype(jnp.bfloat16)
    weight_terms = jnp.einsum(
        "vi,rvj->rij", layer_input[0], aggregated, preferred_element_type=jnp.float32
    )
    rel_weight_grad = lax.psum_scatter(weight_terms, "node", scatter_dimension=1, tiled=True)
    own_rows = lax.psum_scatter(
        jnp.einsum("rvj,rij->vi", aggregated, rel_weights, preferred_element_type=jnp.float32),
        "rel",
        scatter_dimension=0,
        tiled=True,
    )
    self_term = jnp.einsum(
        "vj,ij->vi", out_adjoint[0], self_weight, preferred_element_type=jnp.float32
    )
    d_source = (own_rows + self_term).astype(jnp.bfloat16)[None]
    return (rel_weight_grad, d_source)


def solution(mesh):
    return jax.shard_map(
        on_device,
        mesh=mesh,
        in_specs=(
            P("node", "rel", None),
            P("node", None, None),
            P("rel", None, None),
            P(),
            P("rel", "node", None, None),
            P("rel", "node"),
            P("rel", "node"),
            P("rel", "node"),
            P("rel", "node", None),
        ),
        out_specs=(P("rel", "node", None), P("node", "rel", None)),
        check_vma=False,
    )
```

profile of v0, /device:TPU:32, one launch (start us, length us, event | category | flops | bytes accessed | tf_op | source)
XLA Modules:
  0.0 511.2 jit_solution(1792230578648732150)
XLA Ops:
  7.2 0.7 all-gather.3.cloned.1.call-update
  8.0 52.8 %all-gather.3.cloned.1.call-done = bf16[1,1024,512]{2,1,0:T(8,128)(2,1)} async-done(((bf16[1,64,512]{2,1,0:T(8,128)(2,1)}), bf16[1,1024,512]{2,1,0:T(8,128)(2,1)}) %all-gather.3.cloned.1.call-update) | async-done | bytes 1048592 | tf_op jit(solution)/shard_map/all_gather | solution.py:27
  60.8 0.9 convert_reduce_fusion
  61.7 0.7 multiply_add_fusion
  62.4 0.7 add_bitcast_fusion
  63.1 0.1 select_reduce_fusion
  63.2 0.7 all_to_all.9
  63.9 7.5 %all-to-all-start = ((s32[16,1,8]{2,1,0:T(1,128)}), s32[16,1,8]{2,1,0:T(1,128)S(1)}, u32[]{:S(2)}, u32[]{:S(2)}) async-start(s32[16,1,8]{2,1,0:T(1,128)} %bitcast.2), calls=%async_computation | async-start | bytes 16384 | tf_op jit(solution)/shard_map/all_to_all | solution.py:52
  71.4 5.2 %fusion.7 = bf16[16,8,128,128]{3,1,2,0:T(8,128)(2,1)} fusion(bf16[8,8,128,128]{3,2,1,0:T(8,128)(2,1)} %bitcast.43, s32[64]{0:T(128)S(1)} %multiply_add_fusion), kind=kOutput, calls=%fused_computation.8 | convolution fusion | flops 270540800 | bytes 6291712 | tf_op jit(solution)/shard_map/dot_general | solution.py:41
  76.6 0.9 all-to-all-done
  77.5 6.3 %all-to-all-start.1 = ((bf16[16,8,128,128]{3,1,2,0:T(8,128)(2,1)}), bf16[16,8,128,128]{3,1,2,0:T(8,128)(2,1)}, u32[]{:S(2)}, u32[]{:S(2)}) async-start(bf16[16,8,128,128]{3,1,2,0:T(8,128)(2,1)} %fusion.7), calls=%async_computation.1 | async-start | bytes 8388608 | tf_op jit(solution)/shard_map/all_to_all | solution.py:51
  83.8 0.5 broadcast.300
  84.4 0.7 reduce.5
  85.0 0.1 reshape.241
  85.1 0.1 reshape.245
  85.3 135.1 %all-to-all-done.1 = bf16[16,8,128,128]{3,1,2,0:T(8,128)(2,1)} async-done(((bf16[16,8,128,128]{3,1,2,0:T(8,128)(2,1)}), bf16[16,8,128,128]{3,1,2,0:T(8,128)(2,1)}, u32[]{:S(2)}, u32[]{:S(2)}) %all-to-all-start.1) | async-done | bytes 4194336 | tf_op jit(solution)/shard_map/all_to_all | solution.py:51
  220.4 6.9 %copy.23 = bf16[16,8,128,128]{2,3,1,0:T(8,128)(2,1)} copy(bf16[16,8,128,128]{3,1,2,0:T(8,128)(2,1)} %all-to-all-done.1) | data formatting | bytes 8388608 | tf_op jit(solution)/shard_map/all_to_all | solution.py:51
  227.3 18.1 %all-gather.5.cloned.1.call-done = bf16[16,1024,512]{2,1,0:T(8,128)(2,1)} async-done(((bf16[1,1024,512]{2,1,0:T(8,128)(2,1)}), bf16[16,1024,512]{2,1,0:T(8,128)(2,1)}) %all-gather.5.cloned.1.call-update) | async-done | bytes 16777232 | tf_op jit(solution)/shard_map/all_gather | solution.py:39
  245.4 14.1 %gather_fusion = bf16[128,128,512]{2,1,0:T(8,128)(2,1)} fusion(bf16[128,128,512]{2,1,0:T(8,128)(2,1)} %bitcast.42, s32[1024]{0:T(1024)S(1)} %pad_clamp_fusion), kind=kCustom, calls=%fused_computation | custom fusion | bytes 33554944 | tf_op jit(solution)/shard_map/jit(_take)/gather | solution.py:58
  259.5 15.7 %fusion.3 = bf16[128,128,512]{2,1,0:T(8,128)(2,1)} fusion(bf16[128,128,128]{1,2,0:T(8,128)(2,1)} %bitcast.41, bf16[128,128,512]{2,1,0:T(8,128)(2,1)} %gather_fusion, pred[128]{0:T(512)(128)(4,1)S(1)} %compare_and_fusion), kind=kOutput, calls=%fused_computation.6 | convolution fusion | flops 2164260864 | bytes 37748864 | tf_op jit(solution)/shard_map/sij,sid->sjd/dot_general | solution.py:63
  275.2 15.8 %copy.29 = bf16[16,8,128,512]{3,1,2,0:T(8,128)(2,1)S(1)} copy(bf16[16,8,128,512]{3,2,1,0:T(8,128)(2,1)} %bitcast.39) | data formatting | bytes 33554432
  291.1 2.6 convolution_convert_fusion
  293.7 2.0 convert_element_type.25
  295.7 4.2 convolution_bitcast_fusion.1
  299.9 4.2 copy.25
  304.2 3.8 convolution_bitcast_fusion
  308.1 0.6 dynamic-slice
  309.3 107.4 %all-reduce.3.cloned.1.call-done = f32[2,512,512]{2,0,1:T(2,128)} async-done(((f32[2,512,512]{2,0,1:T(2,128)}), f32[2,512,512]{2,0,1:T(2,128)}) %all-reduce.3.cloned.1.call-update) | async-done | bytes 2097168
  416.8 0.9 constant_dynamic-slice_fusion
  417.7 0.7 copy.26
  418.4 84.3 %reduce-scatter.2.cloned.1.call-done = f32[64,512]{1,0:T(8,128)} async-done(((f32[1024,512]{1,0:T(8,128)}), f32[64,512]{1,0:T(8,128)}) %reduce-scatter.2.cloned.1.call-update) | async-done | bytes 131088 | tf_op jit(solution)/shard_map/reduce_scatter | solution.py:82
  502.7 2.0 fusion.11
  (19 shorter events, 0.3 us)
Async XLA Ops:
  7.2 288.5 %copy-start = (bf16[1,1024,512]{2,1,0:T(8,128)(2,1)S(1)}, bf16[1,1024,512]{2,1,0:T(8,128)(2,1)}, u32[]{:S(2)}) copy-start(bf16[1,1024,512]{2,1,0:T(8,128)(2,1)} %param.10) | copy-start | bytes 3145732
  7.2 53.6 %all-gather.3.cloned.1.call-start = ((), (), s32[]{:S(2)}) async-start(), calls=%async_computation.3 | async-start | bytes 1114112 | tf_op jit(solution)/shard_map/all_gather | solution.py:27
  7.9 237.5 %all-gather.5.cloned.1.call-start = ((), (), s32[]{:S(2)}) async-start(), calls=%async_computation.4 | async-start | bytes 17825792 | tf_op jit(solution)/shard_map/all_gather | solution.py:39
  63.9 13.6 %all-to-all-start = ((s32[16,1,8]{2,1,0:T(1,128)}), s32[16,1,8]{2,1,0:T(1,128)S(1)}, u32[]{:S(2)}, u32[]{:S(2)}) async-start(s32[16,1,8]{2,1,0:T(1,128)} %bitcast.2), calls=%async_computation | async-start | bytes 16384 | tf_op jit(solution)/shard_map/all_to_all | solution.py:52
  77.5 142.9 %all-to-all-start.1 = ((bf16[16,8,128,128]{3,1,2,0:T(8,128)(2,1)}), bf16[16,8,128,128]{3,1,2,0:T(8,128)(2,1)}, u32[]{:S(2)}, u32[]{:S(2)}) async-start(bf16[16,8,128,128]{3,1,2,0:T(8,128)(2,1)} %fusion.7), calls=%async_computation.1 | async-start | bytes 8388608 | tf_op jit(solution)/shard_map/all_to_all | solution.py:51
  83.8 333.0 %all-reduce.3.cloned.1.call-start = ((), (), s32[]{:S(2)}) async-start(), calls=%async_computation.6 | async-start | bytes 4194304
  299.9 4.4 copy-start.1
  304.2 3.9 copy-start.3
  304.2 198.5 %copy-start.2 = (bf16[1,64,512]{2,1,0:T(8,128)(2,1)S(1)}, bf16[1,64,512]{2,1,0:T(8,128)(2,1)}, u32[]{:S(2)}) copy-start(bf16[1,64,512]{2,1,0:T(8,128)(2,1)} %param.9) | copy-start | bytes 196612
  304.2 198.5 %reduce-scatter.2.cloned.1.call-start = ((), (), s32[]{:S(2)}) async-start(), calls=%async_computation.5 | async-start | bytes 2228224 | tf_op jit(solution)/shard_map/reduce_scatter | solution.py:82
Sparse Core Ops, SparseCore 0:
  10.4 50.3 all-gather.2
  62.6 182.7 all-gather.4
  304.3 112.4 all-reduce.2
  420.2 82.4 reduce-scatter.1
where the time goes:
time: 512 us; the launch traced here: 511 us
  waiting for transfers between devices  399 us (78%)
  local copies, waits for them, and re-layouts  46.6 us (9%)
  matrix products  33.5 us (7%)
  between operations  14.5 us (3%)
  starting transfers between devices  13.9 us (3%)
    all_to_all x1, waiting for transfers between devices, on_device(): lax.all_to_all(outgoing, 'node', split_axis=0, concat_axis=0, tiled=True)  135 us
    unnamed x5, waiting for transfers between devices  108 us
    reduce_scatter x1, waiting for transfers between devices, on_device(): lax.psum_scatter(jnp.einsum('rvj,rij->vi', aggregated, rel_weights, prefe...  84.3 us
    all_gather x1, waiting for transfers between devices, on_device(): adjoint = lax.all_gather(out_adjoint, 'rel', axis=1, tiled=True)[0]  52.8 us
    all_gather x1, waiting for transfers between devices, on_device(): group_rows = lax.all_gather(adjoint[None], 'node', axis=0, tiled=True)  18.1 us
    unnamed x12, local copies, waits for them, and re-layouts  18.1 us
    dot_general x1, matrix products, on_device(): jnp.einsum('sij,sid->sjd', got_tiles.reshape(slot_count, tile_edge, tile_...  15.7 us
    gather x1, local copies, waits for them, and re-layouts, on_device(): jnp.take(group_rows.reshape(shard_count * blocks, tile_edge, feature), se...  14.1 us
  transfers between devices with their start and end apart: 6, of which 6 were waited for; matrix products, arithmetic and copies ran while one was open for 4% of the time, Pallas kernels for 0%

commit v1 on v0

--- a/solution.py
+++ b/solution.py
@@ -36,7 +36,9 @@
     slot_of = owners * capacity + position
     placed = jnp.arange(slot_count)[:, None] == slot_of[None, :]
     placing = placed.astype(jnp.bfloat16)
-    group_rows = lax.all_gather(adjoint[None], "node", axis=0, tiled=True)
+    group_rows = jnp.concatenate(
+        lax.all_to_all(jnp.stack([adjoint[None]] * lax.axis_size("node")), "node", 0, 0), axis=0
+    )
     packed = relation * (blocks * blocks) + target * blocks + source
     outgoing = jnp.dot(
         placing,

time: 512 us -> 767 us (1.50)
  waiting for transfers between devices: 399 us -> 640 us
  starting transfers between devices: 13.9 us -> 21.8 us
    all_to_all x0 -> x1, waiting for transfers between devices: none -> 354 us  [on_device(): lax.all_to_all(jnp.stack([adjoint[None]] * lax.axis_size('node')), 'node'...]
    all_to_all x1, waiting for transfers between devices: 135 us -> 40.3 us  [on_device(): lax.all_to_all(outgoing, 'node', split_axis=0, concat_axis=0, tiled=True)]
    all_gather x1 -> x0, waiting for transfers between devices: 18.1 us -> none  [on_device(): group_rows = lax.all_gather(adjoint[None], 'node', axis=0, tiled=True)]
    unnamed x5 -> x4, waiting for transfers between devices: 108 us -> 109 us
  transfers between devices with their start and end apart: 6 -> 6, of which waited for: 6 -> 6; matrix products, arithmetic and copies ran while one was open for 4% -> 3% of each run, Pallas kernels for 0% -> 0%
where the time goes in v1:
time: 767 us
  waiting for transfers between devices  640 us (83%)
  local copies, waits for them, and re-layouts  53.3 us (7%)
  matrix products  33.5 us (4%)
  starting transfers between devices  21.8 us (3%)
  between operations  14.5 us (2%)
    all_to_all x1, waiting for transfers between devices, on_device(): lax.all_to_all(jnp.stack([adjoint[None]] * lax.axis_size('node')), 'node'...  354 us
    unnamed x4, waiting for transfers between devices  109 us
    reduce_scatter x1, waiting for transfers between devices, on_device(): lax.psum_scatter(jnp.einsum('rvj,rij->vi', aggregated, rel_weights, prefe...  84.4 us
    all_gather x1, waiting for transfers between devices, on_device(): adjoint = lax.all_gather(out_adjoint, 'rel', axis=1, tiled=True)[0]  51.4 us
    all_to_all x1, waiting for transfers between devices, on_device(): lax.all_to_all(outgoing, 'node', split_axis=0, concat_axis=0, tiled=True)  40.3 us
    unnamed x12, local copies, waits for them, and re-layouts  18.1 us
    dot_general x1, matrix products, on_device(): jnp.einsum('sij,sid->sjd', got_tiles.reshape(slot_count, tile_edge, tile_...  15.7 us
  transfers between devices with their start and end apart: 6, of which 6 were waited for; matrix products, arithmetic and copies ran while one was open for 3% of the time, Pallas kernels for 0%

profile of v1, /device:TPU:32, one launch (start us, length us, event | category | flops | bytes accessed | tf_op | source)
XLA Modules:
  0.0 766.7 jit_solution(11467968465472710550)
XLA Ops:
  7.2 0.9 convert_reduce_fusion
  8.1 0.7 multiply_add_fusion
  8.8 0.7 add_bitcast_fusion
  9.5 0.1 select_reduce_fusion
  9.6 0.7 all_to_all.12
  10.3 8.6 %all-to-all-start = ((s32[16,1,8]{2,1,0:T(1,128)}), s32[16,1,8]{2,1,0:T(1,128)S(1)}, u32[]{:S(2)}, u32[]{:S(2)}) async-start(s32[16,1,8]{2,1,0:T(1,128)} %bitcast.2), calls=%async_computation | async-start | bytes 16384 | tf_op jit(solution)/shard_map/all_to_all | solution.py:54
  18.9 5.1 fusion.7
  24.0 1.0 all-to-all-done
  25.0 6.3 all-to-all-start.1
  31.3 0.7 all-gather.2.cloned.1.call-update
  32.0 51.4 %all-gather.2.cloned.1.call-done = bf16[1,1024,512]{2,1,0:T(8,128)(2,1)} async-done(((bf16[1,64,512]{2,1,0:T(8,128)(2,1)}), bf16[1,1024,512]{2,1,0:T(8,128)(2,1)}) %all-gather.2.cloned.1.call-update) | async-done | bytes 1048592 | tf_op jit(solution)/shard_map/all_gather | solution.py:27
  83.4 40.3 %all-to-all-done.1 = bf16[16,8,128,128]{3,1,2,0:T(8,128)(2,1)} async-done(((bf16[16,8,128,128]{3,1,2,0:T(8,128)(2,1)}), bf16[16,8,128,128]{3,1,2,0:T(8,128)(2,1)}, u32[]{:S(2)}, u32[]{:S(2)}) %all-to-all-start.1) | async-done | bytes 4194336 | tf_op jit(solution)/shard_map/all_to_all | solution.py:53
  123.7 6.8 stack.3
  130.5 6.9 all-to-all-start.2
  137.4 0.5 broadcast.303
  137.9 0.7 reduce.5
  138.8 6.8 copy.23
  145.7 354.5 %all-to-all-done.2 = bf16[16,1,1024,512]{3,2,1,0:T(8,128)(2,1)} async-done(((bf16[16,1,1024,512]{3,2,1,0:T(8,128)(2,1)}), bf16[16,1,1024,512]{3,2,1,0:T(8,128)(2,1)}, u32[]{:S(2)}, u32[]{:S(2)}) %all-to-all-start.2) | async-done | bytes 16777248 | tf_op jit(solution)/shard_map/all_to_all | solution.py:40
  500.2 14.1 %gather_fusion = bf16[128,128,512]{2,1,0:T(8,128)(2,1)} fusion(bf16[128,128,512]{2,1,0:T(8,128)(2,1)} %bitcast.6, s32[1024]{0:T(1024)S(1)} %pad_clamp_fusion), kind=kCustom, calls=%fused_computation | custom fusion | bytes 33554944 | tf_op jit(solution)/shard_map/jit(_take)/gather | solution.py:60
  514.2 15.7 %fusion.3 = bf16[128,128,512]{2,1,0:T(8,128)(2,1)} fusion(bf16[128,128,128]{1,2,0:T(8,128)(2,1)} %bitcast.42, bf16[128,128,512]{2,1,0:T(8,128)(2,1)} %gather_fusion, pred[128]{0:T(512)(128)(4,1)S(1)} %compare_and_fusion), kind=kOutput, calls=%fused_computation.6 | convolution fusion | flops 2164260864 | bytes 37748864 | tf_op jit(solution)/shard_map/sij,sid->sjd/dot_general | solution.py:65
  530.0 15.8 %copy.29 = bf16[16,8,128,512]{3,1,2,0:T(8,128)(2,1)S(1)} copy(bf16[16,8,128,512]{3,2,1,0:T(8,128)(2,1)} %bitcast.40) | data formatting | bytes 33554432
  545.8 2.6 convolution_convert_fusion
  548.5 2.0 convert_element_type.25
  550.5 4.2 convolution_bitcast_fusion.1
  554.6 4.3 copy.25
  559.0 3.8 convolution_bitcast_fusion
  562.9 0.6 dynamic-slice
  564.1 108.0 %all-reduce.3.cloned.1.call-done = f32[2,512,512]{2,0,1:T(2,128)} async-done(((f32[2,512,512]{2,0,1:T(2,128)}), f32[2,512,512]{2,0,1:T(2,128)}) %all-reduce.3.cloned.1.call-update) | async-done | bytes 2097168
  672.2 0.9 constant_dynamic-slice_fusion
  673.1 0.7 copy.26
  673.7 84.4 %reduce-scatter.2.cloned.1.call-done = f32[64,512]{1,0:T(8,128)} async-done(((f32[1024,512]{1,0:T(8,128)}), f32[64,512]{1,0:T(8,128)}) %reduce-scatter.2.cloned.1.call-update) | async-done | bytes 131088 | tf_op jit(solution)/shard_map/reduce_scatter | solution.py:84
  758.2 2.0 fusion.11
  (19 shorter events, 0.4 us)
Async XLA Ops:
  7.2 543.3 %copy-start = (bf16[1,1024,512]{2,1,0:T(8,128)(2,1)S(1)}, bf16[1,1024,512]{2,1,0:T(8,128)(2,1)}, u32[]{:S(2)}) copy-start(bf16[1,1024,512]{2,1,0:T(8,128)(2,1)} %param.10) | copy-start | bytes 3145732
  10.3 14.7 %all-to-all-start = ((s32[16,1,8]{2,1,0:T(1,128)}), s32[16,1,8]{2,1,0:T(1,128)S(1)}, u32[]{:S(2)}, u32[]{:S(2)}) async-start(s32[16,1,8]{2,1,0:T(1,128)} %bitcast.2), calls=%async_computation | async-start | bytes 16384 | tf_op jit(solution)/shard_map/all_to_all | solution.py:54
  25.0 98.7 %all-to-all-start.1 = ((bf16[16,8,128,128]{3,1,2,0:T(8,128)(2,1)}), bf16[16,8,128,128]{3,1,2,0:T(8,128)(2,1)}, u32[]{:S(2)}, u32[]{:S(2)}) async-start(bf16[16,8,128,128]{3,1,2,0:T(8,128)(2,1)} %fusion.7), calls=%async_computation.1 | async-start | bytes 8388608 | tf_op jit(solution)/shard_map/all_to_all | solution.py:53
  31.2 52.1 %all-gather.2.cloned.1.call-start = ((), (), s32[]{:S(2)}) async-start(), calls=%async_computation.4 | async-start | bytes 1114112 | tf_op jit(solution)/shard_map/all_gather | solution.py:27
  130.5 369.7 %all-to-all-start.2 = ((bf16[16,1,1024,512]{3,2,1,0:T(8,128)(2,1)}), bf16[16,1,1024,512]{3,2,1,0:T(8,128)(2,1)}, u32[]{:S(2)}, u32[]{:S(2)}) async-start(bf16[16,1,1024,512]{3,2,1,0:T(8,128)(2,1)} %stack.3), calls=%async_computation.2 | async-start | bytes 33554432 | tf_op jit(solution)/shard_map/all_to_all | solution.py:40
  137.3 534.8 %all-reduce.3.cloned.1.call-start = ((), (), s32[]{:S(2)}) async-start(), calls=%async_computation.6 | async-start | bytes 4194304
  554.6 4.4 copy-start.1
  558.9 3.9 copy-start.3
  558.9 199.3 %copy-start.2 = (bf16[1,64,512]{2,1,0:T(8,128)(2,1)S(1)}, bf16[1,64,512]{2,1,0:T(8,128)(2,1)}, u32[]{:S(2)}) copy-start(bf16[1,64,512]{2,1,0:T(8,128)(2,1)} %param.9) | copy-start | bytes 196612
  558.9 199.2 %reduce-scatter.2.cloned.1.call-start = ((), (), s32[]{:S(2)}) async-start(), calls=%async_computation.5 | async-start | bytes 2228224 | tf_op jit(solution)/shard_map/reduce_scatter | solution.py:84
Sparse Core Ops, SparseCore 0:
  34.5 48.8 all-gather.1
  559.0 113.0 all-reduce.2
  675.7 82.4 reduce-scatter.1
